TPU v7x, 128 devices: a whole 4x4x4 slice. The times are simulated.
128 devices in a mesh: stu: 8 (over y, core), tea: 16 (over z, x).
Axes of the slice: x: 4, y: 4, z: 4, core: 2. Of those that a mesh axis runs over, the one named last changes fastest.
Arguments:
- student: bfloat16 [16384, 2048], P('stu', 'tea'), may hold values from -8 to 8
- teacher: bfloat16 [16384, 2048], P('tea', 'stu'), may hold values from -8 to 8
- band_start: int32 [32], replicated, may hold values from 0 to 28, as said below
Outputs:
- grad_student: float32 [16384, 2048], P('stu', 'tea')
- stu_pot: float32 [16384], P('stu')
- tea_pot: float32 [16384], P('tea')
- loss: float32 [], replicated
Inputs may be any that keep to these rules, and one draw needn't show every extreme that they name: student block a is paired with teacher blocks band_start[a] to band_start[a] + 3; every teacher block is paired with at least one student block, block 0 with student block 0.
All inputs are finite; a program needn't handle non-finite values.
Results may differ from a plain program's by a relative error of at most 0.002.
Values may be sent and summed in bfloat16 or wider, within the bound.
A program may use at most 192 MiB of HBM per device.

v0:
```python
import functools
import math

import jax
import jax.numpy as jnp
from jax import lax
from jax.experimental import pallas as pl
from jax.experimental.pallas import tpu as pltpu
from jax.sharding import PartitionSpec as P

D = 2048
BLK = 512
W = 4
ITERS = 3
LANES = 128
OWNED = 2048
ROWS = 1024
COLS = 2048
PIECE = 1024
TILES = COLS // LANES
LINES = ROWS // LANES
TOKENS = 16384
GA, GB = 768, 256
QA, QB = 640, 384
WIRES = 300
UP, DOWN = 1, 3

epsilon = 0.02
kappa = math.log2(math.e) / epsilon
log2e = math.log2(math.e)
log2_tokens = math.log2(TOKENS)
unlisted = -1e30
MESH = pl.DeviceIdType.MESH
f32 = jnp.float32
bf16 = jnp.bfloat16


def aligned(start, size):
    return pl.ds(pl.multiple_of(start, size), size)


def total_of(parts):
    return functools.reduce(lambda a, b: a + b, parts)


def merge(parts):
    highest = functools.reduce(jnp.maximum, parts)
    return highest + jnp.log(total_of([jnp.exp2(p - highest) for p in parts])) * log2e


class Place:
    def __init__(self):
        self.s = lax.axis_index("stu")
        self.t = lax.axis_index("tea")
        self.y = lax.div(self.s, 2)
        self.core = lax.rem(self.s, 2)
        self.z = lax.div(self.t, 4)
        self.x = lax.rem(self.t, 4)
        self.h = lax.rem(self.x, 2)
        self.l = lax.div(self.x, 2)
        self.row_slot = 2 * self.z + self.l
        self.col_slot = 2 * self.s + self.h

    def zi(self, dz):
        return lax.rem(self.z + dz, 4)

    def yi(self, dy):
        return lax.rem(self.y + dy, 4)

    def xi(self, dx):
        return lax.rem(self.x + dx, 4)

    def tea(self, dz, dx):
        return self.zi(dz) * 4 + self.xi(dx)

    def stu(self, dy):
        return lax.rem(self.y + dy, 4) * 2 + self.core

    def at_x(self, d):
        return (self.s, self.tea(0, d))

    def at_z(self, d):
        return (self.s, self.tea(d, 0))

    def at_y(self, d):
        return (self.stu(d), self.t)

    def sibling(self):
        return (self.y * 2 + 1 - self.core, self.t)

    def partner(self):
        return (self.s, self.z * 4 + self.l * 2 + 1 - self.h)

    def outer(self):
        return (self.s, self.z * 4 + lax.rem(self.x + 3 + 2 * self.h, 4))

    def at_row(self, d):
        k = lax.rem(self.row_slot + d, 8)
        return (self.s, lax.div(k, 2) * 4 + lax.rem(k, 2) * 2 + self.h)

    def at_col(self, d):
        k = lax.rem(self.col_slot + d, 16)
        return (lax.div(k, 2), self.z * 4 + self.l * 2 + lax.rem(k, 2))


class Wire:
    def __init__(self, send, recv):
        self.send, self.recv, self.used, self.open = send, recv, 0, []

    def start(self, src, dst, device):
        copy = pltpu.make_async_remote_copy(
            src_ref=src, dst_ref=dst,
            send_sem=self.send.at[self.used], recv_sem=self.recv.at[self.used],
            device_id=device, device_id_type=MESH,
        )
        self.used += 1
        copy.start()
        self.open.append(copy)
        return copy

    def drain(self):
        for copy in self.open:
            copy.wait_send()
        self.open = []


WAYS = ((UP, DOWN, 0), (DOWN, UP, 1))


def gather(me, wire, stu_other, own_here, S, T, X, relay_a, relay_b, part_sq, ysq_row, cost):
    A, B = pl.ds(0, GA), pl.ds(GA, GB)
    a_part = [pl.ds(0, GA // 2), pl.ds(GA // 2, GA // 2)]
    b_part = [pl.ds(GA, GB // 2), pl.ds(GA + GB // 2, GB // 2)]
    x_part = [pl.ds(0, GB // 2), pl.ds(GB // 2, GB // 2)]
    t_part = [pl.ds(0, PIECE // 2), pl.ds(PIECE // 2, PIECE // 2)]

    def push(ref, device):
        return wire.start(ref, ref, device)

    def piece(dz, dx, rows):
        return S.at[me.tea(dz, dx), rows]

    def t_push(dy, e, rows, device):
        return push(T.at[me.stu(dy), e, rows], device)

    own, other = me.h, 1 - me.h
    ty, tyf = {}, {0: [], 1: []}
    tc = {(order, d): [] for order in range(2) for d in (0, UP, DOWN, 2)}

    def t_spread(order, e, parts):
        for keep in parts:
            way = WAYS[keep][0]
            ty[order, way, 0] = t_push(0, e, t_part[keep], me.at_y(way))
        for keep in parts:
            way = WAYS[1 - keep][0]
            ty[order, way, 1] = t_push(0, e, t_part[keep], me.at_y(way))
            tc[order, 0].append(t_push(0, e, t_part[keep], me.sibling()))

    own_here()
    ax, ar, axf, az, azf = {}, {}, {}, {}, []
    bz, bzf, bx, br, bxf = {}, [], {}, {}, {}
    for way, back, keep in WAYS:
        ar[way] = wire.start(S.at[me.t, a_part[keep]], relay_a.at[keep], me.at_x(way))
    t_spread(0, own, (0, 1))
    for way, back, keep in WAYS:
        ax[way] = wire.start(stu_other.at[A], S.at[me.t, A], me.at_x(way))
    tp = [t_push(0, own, t_part[keep], me.partner()) for keep in range(2)]

    def turn_a(dx):
        for way, back, keep in WAYS:
            az[dx, way, 0] = push(piece(0, dx, a_part[keep]), me.at_z(way))
        for way, back, keep in WAYS:
            az[dx, way, 1] = push(piece(0, dx, a_part[1 - keep]), me.at_z(way))

    def turn_b(dz):
        for way, back, keep in WAYS:
            br[dz, way] = wire.start(
                piece(dz, 0, b_part[keep]), relay_b.at[me.zi(dz), keep], me.at_x(way)
            )
        for way in (UP, DOWN):
            bx[dz, way] = wire.start(X.at[me.zi(dz)], piece(dz, 0, B), me.at_x(way))

    turn_a(0)
    own_squares(me, T, part_sq)
    squares = tell(wire, part_sq, me.col_slot, 16, me.at_col)
    for way in (UP, DOWN):
        bz[way] = (push(piece(0, 0, B), me.at_z(way)), push(X.at[me.z], me.at_z(way)))

    for way, back, keep in WAYS:
        ar[way].wait_recv()
        axf[way] = wire.start(relay_a.at[keep], piece(0, back, a_part[keep]), me.at_x(way))
    for way, back, keep in WAYS:
        ax[way].wait_recv()
        turn_a(back)

    def t_relay(order, e):
        for way, back, keep in WAYS:
            ty[order, way, 0].wait_recv()
            tyf[order].append(t_push(back, e, t_part[keep], me.at_y(way)))
        for way, back, keep in WAYS:
            ty[order, way, 1].wait_recv()
            tc[order, back].append(t_push(back, e, pl.ds(0, PIECE), me.sibling()))

    def t_last(order, e):
        for keep, copy in enumerate(tyf[order]):
            copy.wait_recv()
            tc[order, 2].append(t_push(2, e, t_part[keep], me.sibling()))

    for copy in axf.values():
        copy.wait_recv()
    turn_a(2)
    for way, back, keep in WAYS:
        for copy in bz[way]:
            copy.wait_recv()
        bzf.append(push(piece(back, 0, b_part[keep]), me.at_z(way)))
        bzf.append(push(X.at[me.zi(back), x_part[keep]], me.at_z(way)))
    t_relay(0, own)
    for copy in tp:
        copy.wait_recv()
    t_spread(1, other, (0, 1))
    turn_b(0)
    turn_b(DOWN)
    turn_b(UP)
    for copy in bzf:
        copy.wait_recv()
    turn_b(2)

    def b_relay(dz):
        bxf[dz] = []
        for way, back, keep in WAYS:
            br[dz, way].wait_recv()
            bxf[dz].append(
                wire.start(relay_b.at[me.zi(dz), keep], piece(dz, back, b_part[keep]), me.at_x(way))
            )

    def a_relay(dx):
        for way, back, keep in WAYS:
            az[dx, way, 0].wait_recv()
            azf.append(push(piece(back, dx, a_part[keep]), me.at_z(way)))

    def b_here(dz):
        for way in (UP, DOWN):
            bx[dz, way].wait_recv()
        for copy in bxf[dz]:
            copy.wait_recv()

    def t_here(order, *places):
        for d in places:
            for copy in tc[order, d]:
                copy.wait_recv()

    def a_here(*places):
        for dx in places:
            for way in (UP, DOWN):
                az[dx, way, 1].wait_recv()

    a_relay(0)
    t_last(0, own)
    a_relay(DOWN)
    a_relay(UP)
    b_relay(0)
    b_relay(DOWN)
    b_relay(UP)
    t_here(0, 0, UP, DOWN, 2)
    b_here(0)
    cost([me.zi(0)], own, first=True)
    a_relay(2)
    b_relay(2)
    t_relay(1, other)
    a_here(0, UP, DOWN, 2)
    b_here(DOWN)
    b_here(UP)
    cost([me.zi(DOWN), me.zi(UP)], own)
    for copy in azf + squares:
        copy.wait_recv()
    for e in range(2):
        ysq_row[e * PIECE // LANES:(e + 1) * PIECE // LANES, :] = total_of(
            [part_sq[2 * i + e] for i in range(8)]
        )
    b_here(2)
    cost([me.zi(2)], own, last=True, new_rows=True)
    t_last(1, other)
    t_here(1, 0, UP, DOWN)
    cost([me.yi(0), me.yi(DOWN), me.yi(UP)], other, first=True)
    t_here(1, 2)
    cost([me.yi(2)], other, last=True)


def own_squares(me, T, part_sq):
    def block(b, carry):
        rows = aligned(b * LANES, LANES)
        squared = total_of([
            jnp.square(T[me.s, me.h, rows, side * LANES:(side + 1) * LANES].astype(f32))
            for side in range(2)
        ])
        part_sq[me.col_slot, pl.ds(b, 1), :] = jnp.sum(squared.T, axis=0, keepdims=True)
        return carry

    lax.fori_loop(0, PIECE // LANES, block, 0)


def cost_of(me, band, S, T, z, xsq, ysq_row):
    scale = kappa / D

    def cost(groups, e, first=False, last=False, new_rows=False):
        def cols_block(n, carry):
            cols = aligned(n * 256, 256)
            rhs = jnp.concatenate(
                [T[2 * group + i, e, cols, :] for group in groups for i in range(2)], axis=1
            )
            lhs = jnp.concatenate(
                [S[4 * group + i] for group in groups for i in range(4)], axis=1
            )
            prod = lax.dot_general(
                lhs, rhs, (((1,), (1,)), ((), ())), preferred_element_type=f32
            )
            for side in range(2):
                at = e * (TILES // 2) + 2 * n + side
                block = me.row_slot * 4 + e * 2 + lax.div(n, 2)
                for half in range(2):
                    rows = pl.ds(half * BLK, BLK)
                    tile = prod[half * BLK:(half + 1) * BLK, side * LANES:(side + 1) * LANES]
                    tile = tile if first else z[at, rows, :] + tile
                    if last:
                        lowest = band[me.s * 4 + me.h * 2 + half]
                        lowest = jnp.full((BLK, LANES), lowest, jnp.int32)
                        here = jnp.full((BLK, LANES), block, jnp.int32)
                        listed = (here >= lowest) & (here < lowest + W)
                        tile = (2.0 * tile - xsq[rows, :] - ysq_row[pl.ds(at, 1), :]) * scale
                        tile = jnp.where(listed, tile, unlisted)
                    z[at, rows, :] = tile
            return carry

        def squares_block(b, carry):
            rows = aligned(b * LANES, LANES)
            squared = total_of([jnp.square(S[i, rows, :].astype(f32)) for i in range(16)])
            xsq[rows, :] = jnp.broadcast_to(
                jnp.sum(squared, axis=1, keepdims=True), (LANES, LANES)
            )
            return carry

        if new_rows:
            lax.fori_loop(0, LINES, squares_block, 0)
        lax.fori_loop(0, PIECE // 256, cols_block, 0)

    return cost


def spread_lines(compact, tall):
    for c in range(TILES):
        tall[c] = jnp.broadcast_to(compact[c:c + 1, :], (8, LANES))


def row_stats(z, tall, lane_high, lane_total, put):
    def lanes(b, carry):
        for part in range(4):
            rows = aligned(b * 64 + part * 16, 16)
            scores = [z[c, rows, :].reshape(2, 8, LANES) + tall[c][None] for c in range(TILES)]
            high = functools.reduce(jnp.maximum, scores)
            lane_high[rows, :] = high.reshape(16, LANES)
            lane_total[rows, :] = total_of([jnp.exp2(v - high) for v in scores]).reshape(16, LANES)
        return carry

    lax.fori_loop(0, ROWS // 64, lanes, 0)

    def block(b, carry):
        rows = aligned(b * LANES, LANES)
        value = (lane_high[rows, :] + jnp.log(lane_total[rows, :]) * log2e).T
        top = jnp.max(value, axis=0, keepdims=True)
        total = jnp.sum(jnp.exp2(value - top), axis=0, keepdims=True)
        put(b, top + jnp.log(total) * log2e)
        return carry

    lax.fori_loop(0, LINES, block, 0, unroll=True)


def spread_rows(compact, wide):
    def block(b, carry):
        line = jnp.broadcast_to(compact[pl.ds(b, 1), :], (LANES, LANES))
        wide[aligned(b * LANES, LANES), :] = line.T
        return carry

    lax.fori_loop(0, LINES, block, 0, unroll=True)


def col_stats(z, wide, put):
    def tiles(cc, carry):
        highs = [jnp.full((8, LANES), unlisted, f32) for _ in range(4)]
        totals = [jnp.zeros((8, LANES), f32) for _ in range(4)]
        for b in range(ROWS // 64):
            rows = pl.ds(b * 64, 64)
            pot = wide[rows, :]
            for k in range(4):
                scores = (z[cc * 4 + k, rows, :] + pot).reshape(8, 8, LANES)
                new = jnp.maximum(highs[k], jnp.max(scores, axis=0))
                totals[k] = totals[k] * jnp.exp2(highs[k] - new) + jnp.sum(
                    jnp.exp2(scores - new[None]), axis=0
                )
                highs[k] = new
        for k in range(4):
            top = jnp.max(highs[k], axis=0, keepdims=True)
            total = jnp.sum(totals[k] * jnp.exp2(highs[k] - top), axis=0, keepdims=True)
            put(cc * 4 + k, top + jnp.log(total) * log2e)
        return carry

    lax.fori_loop(0, TILES // 4, tiles, 0)


def tell(wire, slots, index, count, peer):
    return [wire.start(slots.at[index], slots.at[index], peer(d)) for d in range(1, count)]


def swap(wire, slots, index, count, peer):
    for copy in tell(wire, slots, index, count, peer):
        copy.wait_recv()


def sweeps(me, wire, z, wide, stu, tea, tall, row_l, col_l, lane_high, lane_total):
    tea[...] = jnp.zeros_like(tea)
    for sweep in range(ITERS):
        rl, cl = row_l.at[sweep], col_l.at[sweep]

        def put_row(b, value):
            rl[me.row_slot, pl.ds(b, 1), :] = value

        spread_lines(tea, tall)
        row_stats(z, tall, lane_high, lane_total, put_row)
        swap(wire, rl, me.row_slot, 8, me.at_row)
        stu[...] = -log2_tokens - merge([rl[i] for i in range(8)])
        spread_rows(stu, wide)

        def put_col(c, value):
            cl[me.col_slot, pl.ds(c, 1), :] = value

        col_stats(z, wide, put_col)
        swap(wire, cl, me.col_slot, 16, me.at_col)
        tea[...] = -log2_tokens - merge([cl[i] for i in range(16)])


def make_plan(me, z, wide, tall, xsq, ysq_tall, w, sum_r, lane_mass, lane_pull):
    def lanes(b, loss):
        for part in range(4):
            rows = aligned(b * 64 + part * 16, 16)
            pot = (wide[rows, :] + log2_tokens).reshape(2, 8, LANES)
            mass, pull = [], []
            for c in range(TILES):
                tile = z[c, rows, :].reshape(2, 8, LANES)
                scaled = jnp.exp2(tile + pot + tall[c][None])
                loss = loss + total_of([scaled[i] * tile[i] for i in range(2)])
                rounded = scaled.reshape(16, LANES).astype(bf16)
                w[rows, c * LANES:(c + 1) * LANES] = rounded
                rounded = rounded.astype(f32).reshape(2, 8, LANES)
                mass.append(rounded)
                pull.append(rounded * (ysq_tall[c][None] + (D / kappa) * tile))
            lane_mass[rows, :] = total_of(mass).reshape(16, LANES)
            lane_pull[rows, :] = total_of(pull).reshape(16, LANES)
        return loss

    loss = lax.fori_loop(0, ROWS // 64, lanes, jnp.zeros((8, LANES), f32))

    def block(b, carry):
        rows = aligned(b * LANES, LANES)
        mass = jnp.sum(lane_mass[rows, :].T, axis=0, keepdims=True)
        pull = jnp.sum(lane_pull[rows, :].T, axis=0, keepdims=True)
        own = xsq[rows, :].T[0:1, :]
        usable = own > 1e-20
        gamma = jnp.where(usable, 0.5 * (mass + pull / jnp.where(usable, own, 1.0)), 0.0)
        wide[rows, :] = jnp.broadcast_to(gamma, (LANES, LANES)).T
        sum_r[me.row_slot, pl.ds(b, 1), :] = mass - gamma
        return carry

    lax.fori_loop(0, LINES, block, 0, unroll=True)
    sum_r[me.row_slot, LINES:LINES + 8, :] = loss


def pull_of(S, T, w, wide, G):
    def pull(q, part):
        def rows_block(rows):
            prod = jnp.dot(
                w[rows, :], T[q].reshape(COLS, 2 * LANES), preferred_element_type=f32
            )
            gamma = wide[rows, :]
            for side in range(2):
                own = S[2 * q + side, rows, :].astype(f32)
                G[2 * q + side, rows, :] = gamma * own - prod[:, side * LANES:(side + 1) * LANES]

        if part == 0:
            def block(r, carry):
                rows_block(aligned(r * (QA // 2), QA // 2))
                return carry

            lax.fori_loop(0, 2, block, 0)
        else:
            rows_block(pl.ds(QA, QB))

    return pull


def add(dst, terms):
    def block(r, carry):
        rows = aligned(r * 64, 64)
        dst[rows, :] = total_of([term[rows, :].astype(f32) for term in terms]).astype(dst.dtype)
        return carry

    lax.fori_loop(0, dst.shape[0] // 64, block, 0)


def in_two(rows):
    return (pl.ds(0, rows // 2), pl.ds(rows // 2, rows // 2))


def reduce_a(me, wire, G, pull, far_out, near_out, far_in, near_in, x_out, x_in, x_relay, x_far):
    PARTS = in_two(QA)

    def value(t):
        return G.at[t, pl.ds(0, QA)]

    def pull_to(dz):
        for k in range(2):
            pull(2 * me.zi(dz) + k, 0)

    pull_to(2)
    far = []
    for j in range(4):
        add(far_out.at[j], [value(me.zi(2) * 4 + j)])
        far.append([
            wire.start(far_out.at[j, PARTS[keep]], far_in.at[j, keep], me.at_z(way))
            for way, back, keep in WAYS
        ])
    yield
    pull_to(UP)
    pull_to(DOWN)
    near = []
    for j in range(4):
        for way, back, keep in WAYS:
            far[j][keep].wait_recv()
            chained, direct = PARTS[keep], PARTS[1 - keep]
            mine = value(me.zi(way) * 4 + j)
            out = near_out.at[keep, j]
            add(out.at[chained], [mine.at[chained], far_in.at[j, keep]])
            add(out.at[direct], [mine.at[direct]])
            near.append(wire.start(out, near_in.at[keep, j], me.at_z(way)))
    yield
    pull_to(0)
    for copy in near:
        copy.wait_recv()
    for j in range(4):
        mine = value(me.z * 4 + j)
        add(mine, [mine, near_in.at[0, j], near_in.at[1, j]])
    add(x_out.at[2], [value(me.tea(0, 2))])
    far = [
        wire.start(x_out.at[2, PARTS[keep]], x_relay.at[keep], me.at_x(way))
        for way, back, keep in WAYS
    ]
    near = []
    for way, back, keep in WAYS:
        add(x_out.at[keep], [value(me.tea(0, way))])
        near.append(wire.start(x_out.at[keep], x_in.at[keep], me.at_x(way)))
    yield
    last = []
    for way, back, keep in WAYS:
        far[keep].wait_recv()
        last.append(wire.start(x_relay.at[keep], x_far.at[PARTS[keep]], me.at_x(way)))
    yield
    for copy in near + last:
        copy.wait_recv()
    yield


def reduce_b(
    me, wire, G, pull, far_out, relay, x_out, x_in, x_far, others,
    z_far_out, z_far_in, z_out, z_in,
):
    PARTS = in_two(QB)
    order = (2, UP, DOWN, 0)

    def value(t):
        return G.at[t, pl.ds(QA, QB)]

    far, near, last = {}, {}, {}
    for dz in order:
        pull(2 * me.zi(dz) + 1 - me.l, 1)
        add(far_out.at[me.zi(dz)], [value(me.tea(dz, 2))])
        far[dz] = [
            wire.start(
                far_out.at[me.zi(dz), PARTS[keep]], relay.at[me.zi(dz), keep], me.at_x(way)
            )
            for way, back, keep in WAYS
        ]
    yield
    for dz in order:
        pull(2 * me.zi(dz) + me.l, 1)
        near[dz] = []
        for way, back, keep in WAYS:
            add(x_out.at[keep, me.zi(dz)], [value(me.tea(dz, way))])
            near[dz].append(
                wire.start(x_out.at[keep, me.zi(dz)], x_in.at[keep, me.zi(dz)], me.at_x(way))
            )
        last[dz] = []
        for way, back, keep in WAYS:
            far[dz][keep].wait_recv()
            last[dz].append(
                wire.start(relay.at[me.zi(dz), keep], x_far.at[me.zi(dz), PARTS[keep]], me.at_x(way))
            )
    yield

    def arrived(dz):
        for copy in near[dz] + last[dz]:
            copy.wait_recv()
        mine, other = value(me.tea(dz, 0)), others.at[me.zi(dz)]
        add(mine, [mine, x_far.at[me.zi(dz)]])
        add(other, [x_in.at[0, me.zi(dz)], x_in.at[1, me.zi(dz)]])
        return mine, other

    z_far = {}
    for i, term in enumerate(arrived(2)):
        add(z_far_out.at[i], [term])
        for way, back, keep in WAYS:
            z_far[i, way] = wire.start(
                z_far_out.at[i, PARTS[keep]], z_far_in.at[i, keep], me.at_z(way)
            )
    yield
    z_near = []
    terms = {way: arrived(way) for way in (UP, DOWN)}
    for i in range(2):
        for way, back, keep in WAYS:
            z_far[i, way].wait_recv()
            chained, direct = PARTS[keep], PARTS[1 - keep]
            term, out = terms[way][i], z_out.at[i, keep]
            add(out.at[chained], [term.at[chained], z_far_in.at[i, keep]])
            add(out.at[direct], [term.at[direct]])
            z_near.append(wire.start(out, z_in.at[i, keep], me.at_z(way)))
    yield
    terms = arrived(0)
    for copy in z_near:
        copy.wait_recv()
    for i, term in enumerate(terms):
        add(term, [term, z_in.at[i, 0], z_in.at[i, 1]])
    yield


def kernel(
    band, stu_in, tea_in, grad_out, stu_out, tea_out, loss,
    S, T, X, stu_other, grad, relay_a, relay_b, z, w, G, wide, xsq, xsq_other, part_sq, ysq_row, stu, tea, tall, ysq_tall,
    row_l, col_l, sum_r, sum_c, pair_f, pair_b, others,
    a_far_out, a_near_out, a_far_in, a_near_in, a_x_out, a_x_in, a_x_relay, a_x_far,
    b_far_out, b_relay, b_x_out, b_x_in, b_x_far, b_z_far_out, b_z_far_in, b_z_out, b_z_in,
    send, recv, here,
):
    me = Place()
    mine = pl.multiple_of(me.h * ROWS, ROWS)
    other = pl.multiple_of((1 - me.h) * ROWS, ROWS)
    loads = [
        pltpu.make_async_copy(tea_in, T.at[me.s, me.h], here.at[0]),
        pltpu.make_async_copy(stu_in.at[pl.ds(mine, ROWS)], S.at[me.t], here.at[1]),
        pltpu.make_async_copy(stu_in.at[pl.ds(other, ROWS)], stu_other, here.at[2]),
        pltpu.make_async_copy(stu_in.at[pl.ds(other + GA, GB)], X.at[me.z], here.at[3]),
    ]
    for copy in loads:
        copy.start()
    barrier = pltpu.get_barrier_semaphore()
    peers = [me.outer()] + [me.at_row(d) for d in range(1, 8)] + [me.at_col(d) for d in range(1, 16)]
    for peer in peers:
        pl.semaphore_signal(barrier, inc=1, device_id=peer, device_id_type=MESH)

    def own_here():
        for copy in loads:
            copy.wait()
        pl.semaphore_wait(barrier, len(peers))

    wire = Wire(send, recv)
    gather(
        me, wire, stu_other, own_here, S, T, X, relay_a, relay_b, part_sq, ysq_row,
        cost_of(me, band, S, T, z, xsq, ysq_row),
    )
    sweeps(me, wire, z, wide, stu, tea, tall, row_l, col_l, G.at[0], G.at[1])
    spread_lines(tea, tall)
    spread_lines(ysq_row, ysq_tall)
    make_plan(me, z, wide, tall, xsq, ysq_tall, w, sum_r, G.at[0], G.at[1])
    sums = tell(wire, sum_r, me.row_slot, 8, me.at_row)
    pair_f[me.h] = stu[...] / kappa
    sums.append(wire.start(pair_f.at[me.h], pair_f.at[me.h], me.partner()))
    tea[...] = tea[...] / kappa
    stores = [
        pltpu.make_async_copy(tea.at[aligned(me.h * LINES, LINES)], tea_out, here.at[4])
    ]
    stores[-1].start()
    pull = pull_of(S, T, w, wide, G)
    first = reduce_a(
        me, wire, G, pull, a_far_out, a_near_out, a_far_in, a_near_in,
        a_x_out, a_x_in, a_x_relay, a_x_far,
    )
    second = reduce_b(
        me, wire, G, pull, b_far_out, b_relay, b_x_out, b_x_in, b_x_far, others,
        b_z_far_out, b_z_far_in, b_z_out, b_z_in,
    )
    steps = [first, second] * 3 + [second, first, second, first]
    for number, step in enumerate(steps):
        next(step)
        if number == 1:
            for copy in sums:
                copy.wait_recv()
            summed = total_of([sum_r[i] for i in range(8)])
            sum_c[me.col_slot] = summed[LINES:, :]
            pair_b[me.h] = summed[:LINES, :]
            sums = tell(wire, sum_c, me.col_slot, 16, me.at_col)
            sums.append(wire.start(pair_b.at[me.h], pair_b.at[me.h], me.partner()))
            stores.append(pltpu.make_async_copy(pair_f, stu_out, here.at[5]))
            stores[-1].start()
        if number == 3:
            for copy in sums:
                copy.wait_recv()
            total = total_of([sum_c[i] for i in range(16)])
            total = jnp.sum(jnp.sum(total, axis=0, keepdims=True), axis=1, keepdims=True)
            loss[...] = total * (-1.0 / (kappa * TOKENS))
            spread_rows(pair_b.at[me.h], xsq)
            spread_rows(pair_b.at[1 - me.h], xsq_other)

    def finish(first_row, rows_total, own_terms, other_terms, at):
        def block(r, carry):
            near = aligned(r * LANES, LANES)
            rows = aligned(first_row + r * LANES, LANES)
            grad[aligned(mine + first_row + r * LANES, LANES), :] = (
                xsq[rows, :] * S[me.t, rows, :].astype(f32)
                + total_of([term[near, :].astype(f32) for term in own_terms])
            )
            grad[aligned(other + first_row + r * LANES, LANES), :] = (
                xsq_other[rows, :] * stu_other[rows, :].astype(f32)
                + total_of([term[near, :].astype(f32) for term in other_terms])
            )
            return carry

        lax.fori_loop(0, rows_total // LANES, block, 0)
        for i, base in enumerate((mine, other)):
            rows = aligned(base + first_row, LANES)
            rows = pl.ds(rows.start, rows_total)
            stores.append(
                pltpu.make_async_copy(grad.at[rows], grad_out.at[rows], here.at[at + i])
            )
            stores[-1].start()

    finish(0, QA, [G.at[me.t, pl.ds(0, QA)], a_x_far], [a_x_in.at[0], a_x_in.at[1]], 6)
    finish(QA, QB, [G.at[me.t, pl.ds(QA, QB)]], [others.at[me.z]], 8)
    wire.drain()
    for copy in stores:
        copy.wait()


def one_device(band_start, student, teacher):
    dma = pltpu.SemaphoreType.DMA
    vmem = pl.BlockSpec(memory_space=pltpu.VMEM)
    anywhere = pl.BlockSpec(memory_space=pl.ANY)

    def wide_bf16(*lead):
        return pltpu.VMEM((*lead, LANES), bf16)

    def wide_f32(*lead):
        return pltpu.VMEM((*lead, LANES), f32)

    scratch = [
        wide_bf16(16, ROWS),
        pltpu.VMEM((8, 2, PIECE, 2 * LANES), bf16),
        wide_bf16(4, GB),
        wide_bf16(ROWS),
        wide_f32(OWNED),
        wide_bf16(2, GA // 2),
        wide_bf16(4, 2, GB // 2),
        wide_f32(TILES, ROWS),
        pltpu.VMEM((ROWS, COLS), bf16),
        wide_f32(16, ROWS),
        wide_f32(ROWS),
        wide_f32(ROWS),
        wide_f32(ROWS),
        wide_f32(16, PIECE // LANES),
        wide_f32(TILES),
        wide_f32(LINES),
        wide_f32(TILES),
        wide_f32(TILES, 8),
        wide_f32(TILES, 8),
        wide_f32(ITERS, 8, LINES),
        wide_f32(ITERS, 16, TILES),
        wide_f32(8, LINES + 8),
        wide_f32(16, 8),
        wide_f32(2, LINES),
        wide_f32(2, LINES),
        wide_f32(4, QB),
        wide_bf16(4, QA), wide_bf16(2, 4, QA), wide_bf16(4, 2, QA // 2), wide_bf16(2, 4, QA),
        wide_bf16(3, QA), wide_bf16(2, QA), wide_bf16(2, QA // 2), wide_bf16(QA),
        wide_bf16(4, QB), wide_bf16(4, 2, QB // 2), wide_bf16(2, 4, QB), wide_bf16(2, 4, QB),
        wide_bf16(4, QB),
        wide_bf16(2, QB), wide_bf16(2, 2, QB // 2), wide_bf16(2, 2, QB), wide_bf16(2, 2, QB),
        dma((WIRES,)),
        dma((WIRES,)),
        dma((10,)),
    ]
    return pl.pallas_call(
        kernel,
        out_shape=(
            jax.ShapeDtypeStruct((OWNED, LANES), f32),
            jax.ShapeDtypeStruct((2, LINES, LANES), f32),
            jax.ShapeDtypeStruct((LINES, LANES), f32),
            jax.ShapeDtypeStruct((1, 1), f32),
        ),
        in_specs=[pl.BlockSpec(memory_space=pltpu.SMEM), anywhere, anywhere],
        out_specs=(anywhere, anywhere, anywhere, vmem),
        scratch_shapes=scratch,
        compiler_params=pltpu.CompilerParams(
            collective_id=0, has_side_effects=True, vmem_limit_bytes=62 * 2**20
        ),
    )(band_start, student, teacher)


def local(student, teacher, band_start):
    grad, stu, tea, loss = one_device(band_start, student, teacher)
    return (grad, stu.reshape(OWNED), tea.reshape(PIECE), loss.reshape(()))


def solution(mesh):
    placed = (P("stu", "tea"), P("tea", "stu"), P())
    return jax.shard_map(
        local,
        mesh=mesh,
        in_specs=placed,
        out_specs=(P("stu", "tea"), P("stu"), P("tea"), P()),
        check_vma=False,
    )
```

profile of v0, /device:TPU:1, one launch (start us, length us, event | category | flops | bytes accessed | tf_op | source)
XLA Modules:
  0.0 155.5 jit_solution(3741905312195011244)
XLA Ops:
  0.6 149.5 %shard_map.66 = (f32[2048,128]{1,0:T(8,128)}, f32[2,8,128]{2,1,0:T(8,128)}, f32[8,128]{1,0:T(8,128)}, f32[1,1]{1,0:T(1,128)}) custom-call(s32[32]{0:T(128)} %band.1, bf16[2048,128]{1,0:T(8,128)(2,1)} %stu_in.1, bf16[1024,256]{1,0:T(8,128)(2,1)} %tea_in.1), custom_call_target="tpu_custom_call" | custom-call | tf_op jit(solution)/shard_map/pallas_call | solution.py:796
  150.2 0.0 copy-start
  150.2 2.3 %copy.11 = f32[2048,128]{1,0:T(8,128)} copy(f32[2048,128]{1,0:T(8,128)} %get-tuple-element.16) | data formatting | bytes 2097152
  152.4 0.0 copy-done
  152.4 0.0 copy-start.1
  152.4 0.6 copy.12
  153.0 0.1 copy-done.1
  153.1 0.6 copy.13
Async XLA Ops:
  150.2 2.3 %copy-start = (f32[2,8,128]{2,1,0:T(8,128)S(1)}, f32[2,8,128]{2,1,0:T(8,128)}, u32[]{:S(2)}) copy-start(f32[2,8,128]{2,1,0:T(8,128)} %get-tuple-element.9) | copy-start | bytes 24580
  152.4 0.7 copy-start.1
where the time goes:
time: 156 us
  Pallas kernels  150 us (96%)
  local copies, waits for them, and re-layouts  3.54 us (2%)
  between operations  2.46 us (2%)
    pallas_call x1, Pallas kernels, one_device(): pl.pallas_call(kernel, out_shape=(jax.ShapeDtypeStruct((OWNED, LANES), f3...  150 us
    unnamed x7, local copies, waits for them, and re-layouts  3.54 us

commit v1 on v0

--- a/solution.py
+++ b/solution.py
@@ -164,7 +164,7 @@
     t_spread(0, own, (0, 1))
     for way, back, keep in WAYS:
         ax[way] = wire.start(stu_other.at[A], S.at[me.t, A], me.at_x(way))
-    tp = [t_push(0, own, t_part[keep], me.partner()) for keep in range(2)]
+    tp = [t_push(0, own, t_part[0], me.partner())]
 
     def turn_a(dx):
         for way, back, keep in WAYS:
@@ -192,11 +192,14 @@
     for way, back, keep in WAYS:
         ax[way].wait_recv()
         turn_a(back)
-
-    def t_relay(order, e):
-        for way, back, keep in WAYS:
-            ty[order, way, 0].wait_recv()
-            tyf[order].append(t_push(back, e, t_part[keep], me.at_y(way)))
+    tp.append(t_push(0, own, t_part[1], me.partner()))
+
+    def t_far(order, e, keep):
+        way, back, _ = WAYS[keep]
+        ty[order, way, 0].wait_recv()
+        tyf[order].append(t_push(back, e, t_part[keep], me.at_y(way)))
+
+    def t_whole(order, e):
         for way, back, keep in WAYS:
             ty[order, way, 1].wait_recv()
             tc[order, back].append(t_push(back, e, pl.ds(0, PIECE), me.sibling()))
@@ -206,18 +209,21 @@
             copy.wait_recv()
             tc[order, 2].append(t_push(2, e, t_part[keep], me.sibling()))
 
-    for copy in axf.values():
-        copy.wait_recv()
-    turn_a(2)
     for way, back, keep in WAYS:
         for copy in bz[way]:
             copy.wait_recv()
         bzf.append(push(piece(back, 0, b_part[keep]), me.at_z(way)))
         bzf.append(push(X.at[me.zi(back), x_part[keep]], me.at_z(way)))
-    t_relay(0, own)
-    for copy in tp:
+    for copy in axf.values():
         copy.wait_recv()
-    t_spread(1, other, (0, 1))
+    turn_a(2)
+    tp[0].wait_recv()
+    t_spread(1, other, (0,))
+    t_far(0, own, 0)
+    t_far(0, own, 1)
+    t_whole(0, own)
+    tp[1].wait_recv()
+    t_spread(1, other, (1,))
     turn_b(0)
     turn_b(DOWN)
     turn_b(UP)
@@ -258,15 +264,17 @@
     t_last(0, own)
     a_relay(DOWN)
     a_relay(UP)
+    t_far(1, other, 0)
     b_relay(0)
     b_relay(DOWN)
     b_relay(UP)
     t_here(0, 0, UP, DOWN, 2)
     b_here(0)
+    a_relay(2)
+    t_far(1, other, 1)
     cost([me.zi(0)], own, first=True)
-    a_relay(2)
     b_relay(2)
-    t_relay(1, other)
+    t_whole(1, other)
     a_here(0, UP, DOWN, 2)
     b_here(DOWN)
     b_here(UP)
@@ -351,7 +359,7 @@
         tall[c] = jnp.broadcast_to(compact[c:c + 1, :], (8, LANES))
 
 
-def row_stats(z, tall, lane_high, lane_total, put):
+def row_stats(z, tall, half, lane_high, lane_total, put):
     def lanes(b, carry):
         for part in range(4):
             rows = aligned(b * 64 + part * 16, 16)
@@ -361,34 +369,35 @@
             lane_total[rows, :] = total_of([jnp.exp2(v - high) for v in scores]).reshape(16, LANES)
         return carry
 
-    lax.fori_loop(0, ROWS // 64, lanes, 0)
+    lax.fori_loop(half * (ROWS // 128), (half + 1) * (ROWS // 128), lanes, 0)
 
     def block(b, carry):
-        rows = aligned(b * LANES, LANES)
+        rows = aligned((half * (LINES // 2) + b) * LANES, LANES)
         value = (lane_high[rows, :] + jnp.log(lane_total[rows, :]) * log2e).T
         top = jnp.max(value, axis=0, keepdims=True)
         total = jnp.sum(jnp.exp2(value - top), axis=0, keepdims=True)
         put(b, top + jnp.log(total) * log2e)
         return carry
 
-    lax.fori_loop(0, LINES, block, 0, unroll=True)
-
-
-def spread_rows(compact, wide):
-    def block(b, carry):
-        line = jnp.broadcast_to(compact[pl.ds(b, 1), :], (LANES, LANES))
-        wide[aligned(b * LANES, LANES), :] = line.T
-        return carry
-
-    lax.fori_loop(0, LINES, block, 0, unroll=True)
-
-
-def col_stats(z, wide, put):
+    lax.fori_loop(0, LINES // 2, block, 0, unroll=True)
+
+
+def spread_rows(compact, wide, first=0, count=LINES):
+    for b in range(first, first + count):
+        line = jnp.broadcast_to(compact[b:b + 1, :], (LANES, LANES))
+        wide[b * LANES:(b + 1) * LANES, :] = line.T
+
+
+def col_stats(z, wide, half, kept, put):
     def tiles(cc, carry):
-        highs = [jnp.full((8, LANES), unlisted, f32) for _ in range(4)]
-        totals = [jnp.zeros((8, LANES), f32) for _ in range(4)]
-        for b in range(ROWS // 64):
-            rows = pl.ds(b * 64, 64)
+        if half == 0:
+            highs = [jnp.full((8, LANES), unlisted, f32) for _ in range(4)]
+            totals = [jnp.zeros((8, LANES), f32) for _ in range(4)]
+        else:
+            highs = [kept[0, cc * 4 + k] for k in range(4)]
+            totals = [kept[1, cc * 4 + k] for k in range(4)]
+        for b in range(ROWS // 128):
+            rows = pl.ds(half * (ROWS // 2) + b * 64, 64)
             pot = wide[rows, :]
             for k in range(4):
                 scores = (z[cc * 4 + k, rows, :] + pot).reshape(8, 8, LANES)
@@ -398,6 +407,10 @@
                 )
                 highs[k] = new
         for k in range(4):
+            if half == 0:
+                kept[0, cc * 4 + k] = highs[k]
+                kept[1, cc * 4 + k] = totals[k]
+                continue
             top = jnp.max(highs[k], axis=0, keepdims=True)
             total = jnp.sum(totals[k] * jnp.exp2(highs[k] - top), axis=0, keepdims=True)
             put(cc * 4 + k, top + jnp.log(total) * log2e)
@@ -415,24 +428,32 @@
         copy.wait_recv()
 
 
-def sweeps(me, wire, z, wide, stu, tea, tall, row_l, col_l, lane_high, lane_total):
+def sweeps(me, wire, z, wide, stu, tea, tall, row_l, col_l, kept, lane_high, lane_total):
     tea[...] = jnp.zeros_like(tea)
     for sweep in range(ITERS):
-        rl, cl = row_l.at[sweep], col_l.at[sweep]
-
-        def put_row(b, value):
-            rl[me.row_slot, pl.ds(b, 1), :] = value
-
         spread_lines(tea, tall)
-        row_stats(z, tall, lane_high, lane_total, put_row)
-        swap(wire, rl, me.row_slot, 8, me.at_row)
-        stu[...] = -log2_tokens - merge([rl[i] for i in range(8)])
-        spread_rows(stu, wide)
+        rows_sent = []
+        for half in range(2):
+            rl = row_l.at[sweep, half]
+
+            def put_row(b, value):
+                rl[me.row_slot, pl.ds(b, 1), :] = value
+
+            row_stats(z, tall, half, lane_high, lane_total, put_row)
+            rows_sent.append(tell(wire, rl, me.row_slot, 8, me.at_row))
+        cl = col_l.at[sweep]
 
         def put_col(c, value):
             cl[me.col_slot, pl.ds(c, 1), :] = value
 
-        col_stats(z, wide, put_col)
+        for half in range(2):
+            rl = row_l.at[sweep, half]
+            for copy in rows_sent[half]:
+                copy.wait_recv()
+            first = half * (LINES // 2)
+            stu[first:first + LINES // 2, :] = -log2_tokens - merge([rl[i] for i in range(8)])
+            spread_rows(stu, wide, first, LINES // 2)
+            col_stats(z, wide, half, kept, put_col)
         swap(wire, cl, me.col_slot, 16, me.at_col)
         tea[...] = -log2_tokens - merge([cl[i] for i in range(16)])
 
@@ -642,7 +663,7 @@
 def kernel(
     band, stu_in, tea_in, grad_out, stu_out, tea_out, loss,
     S, T, X, stu_other, grad, relay_a, relay_b, z, w, G, wide, xsq, xsq_other, part_sq, ysq_row, stu, tea, tall, ysq_tall,
-    row_l, col_l, sum_r, sum_c, pair_f, pair_b, others,
+    kept, row_l, col_l, sum_r, sum_c, pair_f, pair_b, others,
     a_far_out, a_near_out, a_far_in, a_near_in, a_x_out, a_x_in, a_x_relay, a_x_far,
     b_far_out, b_relay, b_x_out, b_x_in, b_x_far, b_z_far_out, b_z_far_in, b_z_out, b_z_in,
     send, recv, here,
@@ -673,7 +694,7 @@
         me, wire, stu_other, own_here, S, T, X, relay_a, relay_b, part_sq, ysq_row,
         cost_of(me, band, S, T, z, xsq, ysq_row),
     )
-    sweeps(me, wire, z, wide, stu, tea, tall, row_l, col_l, G.at[0], G.at[1])
+    sweeps(me, wire, z, wide, stu, tea, tall, row_l, col_l, kept, G.at[0], G.at[1])
     spread_lines(tea, tall)
     spread_lines(ysq_row, ysq_tall)
     make_plan(me, z, wide, tall, xsq, ysq_tall, w, sum_r, G.at[0], G.at[1])
@@ -741,6 +762,7 @@
 
     finish(0, QA, [G.at[me.t, pl.ds(0, QA)], a_x_far], [a_x_in.at[0], a_x_in.at[1]], 6)
     finish(QA, QB, [G.at[me.t, pl.ds(QA, QB)]], [others.at[me.z]], 8)
+    assert wire.used <= WIRES, wire.used
     wire.drain()
     for copy in stores:
         copy.wait()
@@ -777,7 +799,8 @@
         wide_f32(TILES),
         wide_f32(TILES, 8),
         wide_f32(TILES, 8),
-        wide_f32(ITERS, 8, LINES),
+        wide_f32(2, TILES, 8),
+        wide_f32(ITERS, 2, 8, LINES // 2),
         wide_f32(ITERS, 16, TILES),
         wide_f32(8, LINES + 8),
         wide_f32(16, 8),

time: 156 us -> 149 us (0.955)
  Pallas kernels: 150 us -> 143 us
    pallas_call x1, Pallas kernels: 150 us -> 143 us  [one_device(): pl.pallas_call(kernel, out_shape=(jax.ShapeDtypeStruct((OWNED, LANES), f3...]
where the time goes in v1:
time: 149 us
  Pallas kernels  143 us (96%)
  local copies, waits for them, and re-layouts  3.54 us (2%)
  between operations  2.46 us (2%)
    pallas_call x1, Pallas kernels, one_device(): pl.pallas_call(kernel, out_shape=(jax.ShapeDtypeStruct((OWNED, LANES), f3...  143 us
    unnamed x7, local copies, waits for them, and re-layouts  3.54 us

profile of v1, /device:TPU:1, one launch (start us, length us, event | category | flops | bytes accessed | tf_op | source)
XLA Modules:
  0.0 149.0 jit_solution(16594223939050661870)
XLA Ops:
  0.6 143.0 %shard_map.66 = (f32[2048,128]{1,0:T(8,128)}, f32[2,8,128]{2,1,0:T(8,128)}, f32[8,128]{1,0:T(8,128)}, f32[1,1]{1,0:T(1,128)}) custom-call(s32[32]{0:T(128)} %band.1, bf16[2048,128]{1,0:T(8,128)(2,1)} %stu_in.1, bf16[1024,256]{1,0:T(8,128)(2,1)} %tea_in.1), custom_call_target="tpu_custom_call" | custom-call | tf_op jit(solution)/shard_map/pallas_call | solution.py:819
  143.7 0.0 copy-start
  143.7 2.3 %copy.11 = f32[2048,128]{1,0:T(8,128)} copy(f32[2048,128]{1,0:T(8,128)} %get-tuple-element.16) | data formatting | bytes 2097152
  146.0 0.0 copy-done
  146.0 0.0 copy-start.1
  146.0 0.6 copy.12
  146.6 0.1 copy-done.1
  146.6 0.6 copy.13
Async XLA Ops:
  143.7 2.3 %copy-start = (f32[2,8,128]{2,1,0:T(8,128)S(1)}, f32[2,8,128]{2,1,0:T(8,128)}, u32[]{:S(2)}) copy-start(f32[2,8,128]{2,1,0:T(8,128)} %get-tuple-element.9) | copy-start | bytes 24580
  146.0 0.7 copy-start.1

commit v2 on v1

--- a/solution.py
+++ b/solution.py
@@ -21,7 +21,7 @@
 LINES = ROWS // LANES
 TOKENS = 16384
 GA, GB = 768, 256
-QA, QB = 640, 384
+QA, QB = 576, 448
 WIRES = 300
 UP, DOWN = 1, 3
 
@@ -518,12 +518,14 @@
 
 
 def add(dst, terms):
+    size = 96 if dst.shape[0] % 96 == 0 else 112
+
     def block(r, carry):
-        rows = aligned(r * 64, 64)
+        rows = aligned(r * size, size)
         dst[rows, :] = total_of([term[rows, :].astype(f32) for term in terms]).astype(dst.dtype)
         return carry
 
-    lax.fori_loop(0, dst.shape[0] // 64, block, 0)
+    lax.fori_loop(0, dst.shape[0] // size, block, 0)
 
 
 def in_two(rows):
@@ -738,30 +740,33 @@
             spread_rows(pair_b.at[1 - me.h], xsq_other)
 
     def finish(first_row, rows_total, own_terms, other_terms, at):
+        size = 192 if rows_total % 192 == 0 else 224
+
         def block(r, carry):
-            near = aligned(r * LANES, LANES)
-            rows = aligned(first_row + r * LANES, LANES)
-            grad[aligned(mine + first_row + r * LANES, LANES), :] = (
+            near = aligned(r * size, size)
+            rows = pl.ds(pl.multiple_of(first_row + r * size, 32), size)
+            own = pl.ds(pl.multiple_of(mine + first_row + r * size, 32), size)
+            there = pl.ds(pl.multiple_of(other + first_row + r * size, 32), size)
+            grad[own, :] = (
                 xsq[rows, :] * S[me.t, rows, :].astype(f32)
                 + total_of([term[near, :].astype(f32) for term in own_terms])
             )
-            grad[aligned(other + first_row + r * LANES, LANES), :] = (
+            grad[there, :] = (
                 xsq_other[rows, :] * stu_other[rows, :].astype(f32)
                 + total_of([term[near, :].astype(f32) for term in other_terms])
             )
             return carry
 
-        lax.fori_loop(0, rows_total // LANES, block, 0)
+        lax.fori_loop(0, rows_total // size, block, 0)
         for i, base in enumerate((mine, other)):
-            rows = aligned(base + first_row, LANES)
-            rows = pl.ds(rows.start, rows_total)
+            rows = pl.ds(pl.multiple_of(base + first_row, 64), rows_total)
             stores.append(
                 pltpu.make_async_copy(grad.at[rows], grad_out.at[rows], here.at[at + i])
             )
             stores[-1].start()
 
+    finish(QA, QB, [G.at[me.t, pl.ds(QA, QB)]], [others.at[me.z]], 8)
     finish(0, QA, [G.at[me.t, pl.ds(0, QA)], a_x_far], [a_x_in.at[0], a_x_in.at[1]], 6)
-    finish(QA, QB, [G.at[me.t, pl.ds(QA, QB)]], [others.at[me.z]], 8)
     assert wire.used <= WIRES, wire.used
     wire.drain()
     for copy in stores:

time: 149 us -> 148 us (level)
  no operation moved by 1% of the time
where the time goes in v2:
time: 148 us
  Pallas kernels  142 us (96%)
  local copies, waits for them, and re-layouts  3.54 us (2%)
  between operations  2.46 us (2%)
    pallas_call x1, Pallas kernels, one_device(): pl.pallas_call(kernel, out_shape=(jax.ShapeDtypeStruct((OWNED, LANES), f3...  142 us
    unnamed x7, local copies, waits for them, and re-layouts  3.54 us

profile of v2, /device:TPU:1, one launch (start us, length us, event | category | flops | bytes accessed | tf_op | source)
XLA Modules:
  0.0 147.8 jit_solution(5689435517788399179)
XLA Ops:
  0.6 141.8 %shard_map.66 = (f32[2048,128]{1,0:T(8,128)}, f32[2,8,128]{2,1,0:T(8,128)}, f32[8,128]{1,0:T(8,128)}, f32[1,1]{1,0:T(1,128)}) custom-call(s32[32]{0:T(128)} %band.1, bf16[2048,128]{1,0:T(8,128)(2,1)} %stu_in.1, bf16[1024,256]{1,0:T(8,128)(2,1)} %tea_in.1), custom_call_target="tpu_custom_call" | custom-call | tf_op jit(solution)/shard_map/pallas_call | solution.py:824
  142.5 0.0 copy-start
  142.5 2.3 %copy.11 = f32[2048,128]{1,0:T(8,128)} copy(f32[2048,128]{1,0:T(8,128)} %get-tuple-element.16) | data formatting | bytes 2097152
  144.7 0.0 copy-done
  144.7 0.0 copy-start.1
  144.8 0.6 copy.12
  145.4 0.1 copy-done.1
  145.4 0.6 copy.13
Async XLA Ops:
  142.5 2.3 %copy-start = (f32[2,8,128]{2,1,0:T(8,128)S(1)}, f32[2,8,128]{2,1,0:T(8,128)}, u32[]{:S(2)}) copy-start(f32[2,8,128]{2,1,0:T(8,128)} %get-tuple-element.9) | copy-start | bytes 24580
  144.7 0.7 copy-start.1

commit v3 on v2

--- a/solution.py
+++ b/solution.py
@@ -20,7 +20,7 @@
 TILES = COLS // LANES
 LINES = ROWS // LANES
 TOKENS = 16384
-GA, GB = 768, 256
+GA, GB = 896, 128
 QA, QB = 576, 448
 WIRES = 300
 UP, DOWN = 1, 3

time: 148 us -> 149 us (level)
  no operation moved by 1% of the time
where the time goes in v3:
time: 149 us
  Pallas kernels  143 us (96%)
  local copies, waits for them, and re-layouts  3.54 us (2%)
  between operations  2.46 us (2%)
    pallas_call x1, Pallas kernels, one_device(): pl.pallas_call(kernel, out_shape=(jax.ShapeDtypeStruct((OWNED, LANES), f3...  143 us
    unnamed x7, local copies, waits for them, and re-layouts  3.54 us

profile of v3, /device:TPU:1, one launch (start us, length us, event | category | flops | bytes accessed | tf_op | source)
XLA Modules:
  0.0 149.2 jit_solution(6035570814155222824)
XLA Ops:
  0.6 143.2 %shard_map.66 = (f32[2048,128]{1,0:T(8,128)}, f32[2,8,128]{2,1,0:T(8,128)}, f32[8,128]{1,0:T(8,128)}, f32[1,1]{1,0:T(1,128)}) custom-call(s32[32]{0:T(128)} %band.1, bf16[2048,128]{1,0:T(8,128)(2,1)} %stu_in.1, bf16[1024,256]{1,0:T(8,128)(2,1)} %tea_in.1), custom_call_target="tpu_custom_call" | custom-call | tf_op jit(solution)/shard_map/pallas_call | solution.py:824
  143.9 0.0 copy-start
  143.9 2.3 %copy.11 = f32[2048,128]{1,0:T(8,128)} copy(f32[2048,128]{1,0:T(8,128)} %get-tuple-element.16) | data formatting | bytes 2097152
  146.1 0.0 copy-done
  146.1 0.0 copy-start.1
  146.1 0.6 copy.12
  146.7 0.1 copy-done.1
  146.8 0.6 copy.13
Async XLA Ops:
  143.9 2.3 %copy-start = (f32[2,8,128]{2,1,0:T(8,128)S(1)}, f32[2,8,128]{2,1,0:T(8,128)}, u32[]{:S(2)}) copy-start(f32[2,8,128]{2,1,0:T(8,128)} %get-tuple-element.9) | copy-start | bytes 24580
  146.1 0.7 copy-start.1
